TPU v7x, 32 devices: a whole 2x2x4 slice. The times are simulated.
32 devices in a mesh: dom: 16 (over z, y, x), feat: 2 (over core).
Axes of the slice: x: 2, y: 2, z: 4, core: 2. Of those that a mesh axis runs over, the one named last changes fastest.
Arguments:
- features: bfloat16 [32768, 100], P('dom', 'feat'), may hold values from -6 to 6
- local_mask: int32 [32768, 2048], P('dom'), may hold values 0 or 1
- halo_mask: int32 [32768, 128], P('dom'), may hold values 0 or 1
- send_rows: int32 [16, 16, 8], P('dom'), may hold values from 0 to 2047
- labels: int32 [32768], P('dom'), may hold values from 0 to 46
- label_mask: int32 [32768], P('dom'), may hold values from 0 to 1
- master: float32 [2, 103680], P('feat', 'dom')
- first_moment: float32 [2, 103680], P('feat', 'dom'), may hold values from -0.00390625 to 0.00390625
- second_moment: float32 [2, 103680], P('feat', 'dom'), may hold values from 6.866455e-09 to 2.746582e-08
Outputs:
- loss_sum: float32 [], replicated
- label_count: float32 [], replicated
- new_master: float32 [2, 103680], P('feat', 'dom')
- new_first: float32 [2, 103680], P('feat', 'dom')
- new_second: float32 [2, 103680], P('feat', 'dom')
All inputs are finite; a program needn't handle non-finite values. No bound on the sum of `local_mask` or of `halo_mask` on one device may be relied on, other than what follows from the above.
Results may differ from a plain program's by a relative error of at most 0.0005.
The roundings to bfloat16 on the way count: a program that leaves them out, or rounds other values in their place, can miss the bound.
Values may be sent and summed in bfloat16 or wider, within the bound.
A program may use at most 128 MiB of HBM per device.

v0:
```python
import jax
import jax.numpy as jnp
from jax import lax
from jax.sharding import PartitionSpec as P

HID = 256
CLS = 47
STEP = 10
EPSILON = 1e-05
LEARN_RATE = 0.02
DECAY_ONE = 0.9
DECAY_TWO = 0.999
ADAM_EPS = 1e-08
WEIGHT_DECAY = 0.01


def product(matrix_a, matrix_b):
    return jnp.dot(matrix_a, matrix_b, preferred_element_type=jnp.float32)


def contract_rows(matrix_a, matrix_b):
    return lax.dot_general(
        matrix_a, matrix_b, (((0,), (0,)), ((), ())), preferred_element_type=jnp.float32
    )


def contract_cols(matrix_a, matrix_b):
    return lax.dot_general(
        matrix_a, matrix_b, (((1,), (1,)), ((), ())), preferred_element_type=jnp.float32
    )


def unpack(flat_params, inner_width, hidden_width):
    edge_one = 2 * inner_width * HID
    edge_two = edge_one + 2 * hidden_width * HID
    edge_three = edge_two + 2 * hidden_width * CLS
    layer_one = flat_params[:edge_one].reshape(2, inner_width, HID)
    layer_two = flat_params[edge_one:edge_two].reshape(2, hidden_width, HID)
    head_part = flat_params[edge_two:edge_three].reshape(2, hidden_width, CLS)
    norm_part = flat_params[edge_three:].reshape(4, hidden_width)
    matrices = [
        (layer_one[0], layer_one[1]),
        (layer_two[0], layer_two[1]),
        (head_part[0], head_part[1]),
    ]
    return (matrices, norm_part)


def layer_forward(states, weight_pair, graph, is_head):
    local_adj, halo_adj, inverse, send_index = graph
    outgoing = jnp.take(states, send_index, axis=0)
    incoming = lax.all_to_all(outgoing, "dom", split_axis=0, concat_axis=0, tiled=True)
    halo_feats = incoming.reshape(-1, states.shape[1])
    summed = product(local_adj, states) + product(halo_adj, halo_feats)
    aggregated = (summed * inverse[:, None]).astype(jnp.bfloat16)
    if is_head:
        partial_value = product(states, weight_pair[0]) + product(aggregated, weight_pair[1])
        mixed = lax.psum(partial_value, "feat")
    else:
        partial_value = product(states, weight_pair[0]) + product(aggregated, weight_pair[1])
        mixed = lax.psum_scatter(partial_value, "feat", scatter_dimension=1, tiled=True)
    return (mixed, aggregated)


def norm_forward(mixed, gain, shift):
    totals = lax.psum((jnp.sum(mixed, axis=1), jnp.sum(mixed * mixed, axis=1)), "feat")
    centre_mean = totals[0] / HID
    variance = totals[1] / HID - centre_mean * centre_mean
    scale_inv = lax.rsqrt(variance + EPSILON)
    normed = (mixed - centre_mean[:, None]) * scale_inv[:, None]
    shifted = normed * gain + shift
    return (jax.nn.gelu(shifted).astype(jnp.bfloat16), (normed, scale_inv, shifted))


def norm_backward(grad_out, kept, gain):
    normed, scale_inv, shifted = kept
    unused, gelu_back = jax.vjp(jax.nn.gelu, shifted)
    grad_shift = gelu_back(grad_out)[0]
    grad_gain = jnp.sum(grad_shift * normed, axis=0)
    grad_bias = jnp.sum(grad_shift, axis=0)
    grad_normed = grad_shift * gain
    totals = lax.psum((jnp.sum(grad_normed, axis=1), jnp.sum(grad_normed * normed, axis=1)), "feat")
    grad_mixed = scale_inv[:, None] * (
        grad_normed - totals[0][:, None] / HID - normed * totals[1][:, None] / HID
    )
    return (grad_mixed, grad_gain, grad_bias)


def layer_backward(grad_full, states, aggregated, weight_pair, graph, needs_input):
    grad_self = contract_rows(states, grad_full)
    grad_neigh = contract_rows(aggregated, grad_full)
    if not needs_input:
        return (grad_self, grad_neigh, None)
    local_adj, halo_adj, inverse, send_index = graph
    grad_states = contract_cols(grad_full, weight_pair[0])
    grad_agg = contract_cols(grad_full, weight_pair[1])
    grad_summed = (grad_agg * inverse[:, None]).astype(jnp.bfloat16)
    grad_states = grad_states + contract_rows(local_adj, grad_summed)
    grad_halo = contract_rows(halo_adj, grad_summed).astype(jnp.bfloat16)
    returned = lax.all_to_all(
        grad_halo.reshape(send_index.shape + (-1,)), "dom", split_axis=0, concat_axis=0, tiled=True
    )
    flat_back = returned.reshape(-1, returned.shape[-1]).astype(jnp.float32)
    grad_states = grad_states.at[send_index.reshape(-1)].add(flat_back)
    return (grad_self, grad_neigh, grad_states)


def per_device(
    features,
    local_mask,
    halo_mask,
    send_rows,
    labels,
    label_mask,
    master,
    first_moment,
    second_moment,
):
    gathered = lax.all_gather(master.astype(jnp.bfloat16), "dom", axis=1, tiled=True)
    inner_width = features.shape[1]
    hidden_width = HID // lax.axis_size("feat")
    matrices, norm_part = unpack(gathered[0], inner_width, hidden_width)
    norm_float = norm_part.astype(jnp.float32)
    local_adj = local_mask.astype(jnp.bfloat16)
    halo_adj = halo_mask.astype(jnp.bfloat16)
    degree = jnp.sum(local_mask, axis=1) + jnp.sum(halo_mask, axis=1)
    inverse = 1.0 / jnp.maximum(degree, 1).astype(jnp.float32)
    graph = (local_adj, halo_adj, inverse, send_rows[0])
    weight_mask = label_mask.astype(jnp.float32)
    states = features
    inputs_kept = []
    norms_kept = []
    for number in range(3):
        mixed, aggregated = layer_forward(states, matrices[number], graph, number == 2)
        inputs_kept.append((states, aggregated))
        if number < 2:
            states, kept = norm_forward(mixed, norm_float[2 * number], norm_float[2 * number + 1])
            norms_kept.append(kept)
    log_total = jax.nn.logsumexp(mixed, axis=1)
    classes = lax.broadcasted_iota(jnp.int32, mixed.shape, 1)
    onehot = (classes == labels[:, None]).astype(jnp.float32)
    picked = jnp.sum(mixed * onehot, axis=1)
    loss_sum, label_count = lax.psum(
        (jnp.sum((log_total - picked) * weight_mask), jnp.sum(weight_mask)), "dom"
    )
    probs = jnp.exp(mixed - log_total[:, None])
    grad_full = ((probs - onehot) * (weight_mask / label_count)[:, None]).astype(jnp.bfloat16)
    weight_grads = [None, None, None]
    norm_grads = [None, None]
    for number in (2, 1, 0):
        states, aggregated = inputs_kept[number]
        grad_self, grad_neigh, grad_states = layer_backward(
            grad_full, states, aggregated, matrices[number], graph, number > 0
        )
        weight_grads[number] = (grad_self, grad_neigh)
        if number > 0:
            grad_mixed, grad_gain, grad_bias = norm_backward(
                grad_states, norms_kept[number - 1], norm_float[2 * number - 2]
            )
            norm_grads[number - 1] = (grad_gain, grad_bias)
            grad_full = lax.all_gather(grad_mixed.astype(jnp.bfloat16), "feat", axis=1, tiled=True)
    pieces = [
        weight_grads[0][0],
        weight_grads[0][1],
        weight_grads[1][0],
        weight_grads[1][1],
        weight_grads[2][0],
        weight_grads[2][1],
        norm_grads[0][0],
        norm_grads[0][1],
        norm_grads[1][0],
        norm_grads[1][1],
    ]
    gradient = jnp.concatenate([piece.reshape(-1) for piece in pieces])[None, :]
    shard_width = master.shape[1]
    summed_all = lax.psum(gradient, "dom")
    own_grad = lax.dynamic_slice_in_dim(
        summed_all, lax.axis_index("dom") * shard_width, shard_width, 1
    )
    new_first = DECAY_ONE * first_moment + (1.0 - DECAY_ONE) * own_grad
    new_second = DECAY_TWO * second_moment + (1.0 - DECAY_TWO) * own_grad * own_grad
    first_hat = new_first / (1.0 - DECAY_ONE**STEP)
    second_hat = new_second / (1.0 - DECAY_TWO**STEP)
    new_master = master - LEARN_RATE * (
        first_hat / (jnp.sqrt(second_hat) + ADAM_EPS) + WEIGHT_DECAY * master
    )
    return (loss_sum, label_count, new_master, new_first, new_second)


def solution(mesh):
    in_specs = (
        P("dom", "feat"),
        P("dom", None),
        P("dom", None),
        P("dom", None, None),
        P("dom"),
        P("dom"),
        P("feat", "dom"),
        P("feat", "dom"),
        P("feat", "dom"),
    )
    out_specs = (P(), P(), P("feat", "dom"), P("feat", "dom"), P("feat", "dom"))
    return jax.shard_map(
        per_device, mesh=mesh, in_specs=in_specs, out_specs=out_specs, check_vma=False
    )
```

profile of v0, /device:TPU:0, one launch (start us, length us, event | category | flops | bytes accessed | tf_op | source)
XLA Modules:
  0.0 488.4 jit_solution(10697952890645526541)
XLA Ops:
  11.6 8.3 %all-to-all-start = ((bf16[16,2,200]{2,1,0:T(2,128)(2,1)}), bf16[16,2,200]{2,1,0:T(2,128)(2,1)S(1)}, u32[]{:S(2)}, u32[]{:S(2)}) async-start(bf16[16,2,200]{2,1,0:T(2,128)(2,1)} %reshape.262), calls=%async_computation | async-start | bytes 32768 | tf_op jit(solution)/shard_map/all_to_all | solution.py:52
  23.9 13.5 %fusion.39 = (s32[2048]{0:T(1024)S(1)}, bf16[2048,2048]{1,0:T(8,128)(2,1)S(1)}) fusion(s32[2048,2048]{1,0:T(8,128)} %param.12), kind=kLoop, calls=%fused_computation.129 | loop fusion | flops 8386560 | bytes 25174016 | tf_op jit(solution)/shard_map/reduce_sum | solution.py:126
  37.8 2.9 copy-done
  40.7 2.7 fusion.41
  43.9 89.5 %all-reduce.14.cloned.1.call-done = bf16[103680]{0:T(1024)(128)(2,1)} async-done(((bf16[103680]{0:T(1024)(128)(2,1)}), bf16[103680]{0:T(1024)(128)(2,1)}) %all-reduce.14.cloned.1.call-update) | async-done | bytes 207376
  141.3 6.8 %reduce-scatter.3.cloned.1.call-done = f32[2048,128]{0,1:T(8,128)} async-done(((f32[2048,256]{0,1:T(8,128)}), f32[2048,128]{0,1:T(8,128)}) %reduce-scatter.3.cloned.1.call-update) | async-done | bytes 1048592 | tf_op jit(solution)/shard_map/reduce_scatter | solution.py:61
  149.4 3.3 all-reduce.5
  154.6 7.5 %fusion.43 = f32[128,2048]{1,0:T(8,128)} fusion(bf16[2048,128]{0,1:T(8,128)(2,1)S(1)} %multiply_convert_fusion.3, bf16[2048,2048]{1,0:T(8,128)(2,1)} %copy-done), kind=kOutput, calls=%fused_computation.133 | convolution fusion | flops 1073741824 | bytes 9961472 | tf_op jit(solution)/shard_map/dot_general | solution.py:18
  163.8 6.9 %all-to-all-start.1 = ((bf16[16,8,128]{2,1,0:T(8,128)(2,1)}), bf16[16,8,128]{2,1,0:T(8,128)(2,1)S(1)}, u32[]{:S(2)}, u32[]{:S(2)}) async-start(bf16[16,8,128]{2,1,0:T(8,128)(2,1)} %bitcast_select_fusion.1), calls=%async_computation.2 | async-start | bytes 65536 | tf_op jit(solution)/shard_map/all_to_all | solution.py:52
  172.3 5.8 %all-to-all-done.1 = bf16[16,8,128]{2,1,0:T(8,128)(2,1)S(1)} async-done(((bf16[16,8,128]{2,1,0:T(8,128)(2,1)}), bf16[16,8,128]{2,1,0:T(8,128)(2,1)S(1)}, u32[]{:S(2)}, u32[]{:S(2)}) %all-to-all-start.1) | async-done | bytes 32800 | tf_op jit(solution)/shard_map/all_to_all | solution.py:52
  180.5 2.7 convolution_add_fusion.1
  184.6 5.0 %reduce-scatter.5.cloned.1.call-done = f32[2048,128]{0,1:T(8,128)} async-done(((f32[2048,256]{0,1:T(8,128)}), f32[2048,128]{0,1:T(8,128)}) %reduce-scatter.5.cloned.1.call-update) | async-done | bytes 1048592 | tf_op jit(solution)/shard_map/reduce_scatter | solution.py:61
  190.9 3.3 all-reduce.4
  196.1 6.3 %fusion.45 = f32[128,2048]{1,0:T(8,128)S(1)} fusion(bf16[2048,128]{0,1:T(8,128)(2,1)S(1)} %multiply_convert_fusion.2, bf16[2048,2048]{1,0:T(8,128)(2,1)} %copy-done), kind=kOutput, calls=%fused_computation.135 | convolution fusion | flops 1073741824 | bytes 9961472 | tf_op jit(solution)/shard_map/dot_general | solution.py:18
  204.1 6.9 %all-to-all-start.2 = ((bf16[16,8,128]{2,1,0:T(8,128)(2,1)}), bf16[16,8,128]{2,1,0:T(8,128)(2,1)S(1)}, u32[]{:S(2)}, u32[]{:S(2)}) async-start(bf16[16,8,128]{2,1,0:T(8,128)(2,1)} %bitcast_select_fusion), calls=%async_computation.4 | async-start | bytes 65536 | tf_op jit(solution)/shard_map/all_to_all | solution.py:52
  211.2 7.1 %all-to-all-done.2 = bf16[16,8,128]{2,1,0:T(8,128)(2,1)S(1)} async-done(((bf16[16,8,128]{2,1,0:T(8,128)(2,1)}), bf16[16,8,128]{2,1,0:T(8,128)(2,1)S(1)}, u32[]{:S(2)}, u32[]{:S(2)}) %all-to-all-start.2) | async-done | bytes 32800 | tf_op jit(solution)/shard_map/all_to_all | solution.py:52
  220.7 15.0 %all-reduce.10.cloned.1.call-done = f32[2048,47]{0,1:T(8,128)} async-done(((f32[2048,47]{0,1:T(8,128)}), f32[2048,47]{0,1:T(8,128)}) %all-reduce.10.cloned.1.call-update) | async-done | bytes 385040 | tf_op jit(solution)/shard_map/psum | solution.py:58
  238.5 42.6 %all-reduce.1 = (f32[]{:T(128)}, f32[]{:T(128)}) all-reduce(f32[]{:T(128)} %get-tuple-element.27, f32[]{:T(128)} %get-tuple-element.26), channel_id=1, replica_groups=mesh['dom'=16,'feat'=2] {'dom'}, use_global_device_ids=true, to_apply=%region_17.19 | all-reduce | flops 2 | bytes 16 | tf_op jit(solution)/shard_map/psum | solution.py:143
  283.4 7.9 %convolution_bitcast_fusion.2 = f32[2048,128]{1,0:T(8,128)} fusion(bf16[2048,128]{1,0:T(8,128)(2,1)S(1)} %fusion.5, bf16[2048,2048]{1,0:T(8,128)(2,1)} %copy-done), kind=kOutput, calls=%fused_computation.9 | convolution fusion | flops 1073741824 | bytes 9961472 | tf_op jit(solution)/shard_map/dot_general | solution.py:22
  292.2 3.5 all-to-all-start.3
  297.3 5.8 %all-to-all-done.3 = bf16[16,8,128]{2,1,0:T(8,128)(2,1)S(1)} async-done(((bf16[16,8,128]{2,1,0:T(8,128)(2,1)}), bf16[16,8,128]{2,1,0:T(8,128)(2,1)S(1)}, u32[]{:S(2)}, u32[]{:S(2)}) %all-to-all-start.3) | async-done | bytes 32800 | tf_op jit(solution)/shard_map/all_to_all | solution.py:100
  306.4 3.0 multiply_reduce_fusion
  309.3 3.4 all-reduce.3
  313.9 5.7 %all-gather.3.cloned.1.call-done = bf16[2048,256]{0,1:T(8,128)(2,1)} async-done(((bf16[2048,128]{0,1:T(8,128)(2,1)}), bf16[2048,256]{0,1:T(8,128)(2,1)}) %all-gather.3.cloned.1.call-update) | async-done | bytes 1048592 | tf_op jit(solution)/shard_map/all_gather | solution.py:161
  321.6 7.8 %convolution_bitcast_fusion.1 = f32[2048,128]{1,0:T(8,128)} fusion(bf16[2048,128]{1,0:T(8,128)(2,1)S(1)} %fusion.2, bf16[2048,2048]{1,0:T(8,128)(2,1)} %copy-done), kind=kOutput, calls=%fused_computation.8 | convolution fusion | flops 1073741824 | bytes 9961472 | tf_op jit(solution)/shard_map/dot_general | solution.py:22
  330.3 6.9 %all-to-all-start.4 = ((bf16[16,8,128]{2,1,0:T(8,128)(2,1)}), bf16[16,8,128]{2,1,0:T(8,128)(2,1)S(1)}, u32[]{:S(2)}, u32[]{:S(2)}) async-start(bf16[16,8,128]{2,1,0:T(8,128)(2,1)} %fusion.10), calls=%async_computation.6 | async-start | bytes 65536 | tf_op jit(solution)/shard_map/all_to_all | solution.py:100
  337.3 2.7 convolution_add_fusion.5
  340.0 4.6 all-to-all-done.4
  344.7 3.5 scatter_custom_fusion.1
  350.8 3.3 multiply_reduce_fusion.1
  354.1 3.3 all-reduce.2
  370.5 109.5 %all-reduce.12.cloned.1.call-done = f32[1,103680]{1,0:T(1,128)} async-done(((f32[1,103680]{1,0:T(1,128)}), f32[1,103680]{1,0:T(1,128)}) %all-reduce.12.cloned.1.call-update) | async-done | bytes 414736 | tf_op jit(solution)/shard_map/psum | solution.py:176
  (170 shorter events, 66.1 us)
Async XLA Ops:
  11.6 31.8 %all-to-all-start = ((bf16[16,2,200]{2,1,0:T(2,128)(2,1)}), bf16[16,2,200]{2,1,0:T(2,128)(2,1)S(1)}, u32[]{:S(2)}, u32[]{:S(2)}) async-start(bf16[16,2,200]{2,1,0:T(2,128)(2,1)} %reshape.262), calls=%async_computation | async-start | bytes 32768 | tf_op jit(solution)/shard_map/all_to_all | solution.py:52
  19.9 113.5 %all-reduce.14.cloned.1.call-start = ((), (), s32[]{:S(2)}) async-start(), calls=%async_computation.13 | async-start | bytes 417792
  23.8 124.3 %reduce-scatter.3.cloned.1.call-start = ((), (), s32[]{:S(2)}) async-start(), calls=%async_computation.7 | async-start | bytes 3145728 | tf_op jit(solution)/shard_map/reduce_scatter | solution.py:61
  43.3 95.3 %copy-start.16 = (s32[1,16,8]{1,2,0:T(8,128)S(1)}, s32[1,16,8]{1,2,0:T(8,128)}, u32[]{:S(2)}) copy-start(s32[1,16,8]{1,2,0:T(8,128)} %param.14) | copy-start | bytes 1540
  43.9 118.3 %copy-start.9 = (bf16[2048,50]{0,1:T(8,128)(2,1)}, bf16[2048,50]{0,1:T(8,128)(2,1)S(1)}, u32[]{:S(2)}) copy-start(bf16[2048,50]{0,1:T(8,128)(2,1)S(1)} %fusion.8) | copy-start | bytes 614404
  134.6 27.6 %copy-start.10 = (bf16[1,103680]{1,0:T(2,128)(2,1)}, bf16[1,103680]{1,0:T(2,128)(2,1)S(1)}, u32[]{:S(2)}) copy-start(bf16[1,103680]{1,0:T(2,128)(2,1)S(1)} %reshape.240) | copy-start | bytes 622084
  141.3 30.9 %copy-start.21 = (f32[128]{0:T(128)}, f32[128]{0:T(128)S(1)}, u32[]{:S(2)}) copy-start(f32[128]{0:T(128)S(1)} %get-tuple-element.54) | copy-start | bytes 1540
  154.6 28.6 %copy-start.4 = (bf16[2048,128]{0,1:T(8,128)(2,1)}, bf16[2048,128]{0,1:T(8,128)(2,1)S(1)}, u32[]{:S(2)}) copy-start(bf16[2048,128]{0,1:T(8,128)(2,1)S(1)} %multiply_convert_fusion.3) | copy-start | bytes 1572868
  162.4 31.8 %copy-start.23 = (f32[128]{0:T(128)S(1)}, f32[128]{0:T(128)}, u32[]{:S(2)}) copy-start(f32[128]{0:T(128)} %get-tuple-element.53) | copy-start | bytes 1540
  163.8 14.3 %all-to-all-start.1 = ((bf16[16,8,128]{2,1,0:T(8,128)(2,1)}), bf16[16,8,128]{2,1,0:T(8,128)(2,1)S(1)}, u32[]{:S(2)}, u32[]{:S(2)}) async-start(bf16[16,8,128]{2,1,0:T(8,128)(2,1)} %bitcast_select_fusion.1), calls=%async_computation.2 | async-start | bytes 65536 | tf_op jit(solution)/shard_map/all_to_all | solution.py:52
  170.7 18.8 %reduce-scatter.5.cloned.1.call-start = ((), (), s32[]{:S(2)}) async-start(), calls=%async_computation.8 | async-start | bytes 3145728 | tf_op jit(solution)/shard_map/reduce_scatter | solution.py:61
  196.1 40.7 %copy-start.17 = (s32[2048]{0:T(1024)S(1)}, s32[2048]{0:T(1024)}, u32[]{:S(2)}) copy-start(s32[2048]{0:T(1024)} %param.15) | copy-start | bytes 24580
  196.1 41.8 %copy-start.18 = (s32[2048]{0:T(1024)S(1)}, s32[2048]{0:T(1024)}, u32[]{:S(2)}) copy-start(s32[2048]{0:T(1024)} %param.16) | copy-start | bytes 24580
  204.1 14.3 %all-to-all-start.2 = ((bf16[16,8,128]{2,1,0:T(8,128)(2,1)}), bf16[16,8,128]{2,1,0:T(8,128)(2,1)S(1)}, u32[]{:S(2)}, u32[]{:S(2)}) async-start(bf16[16,8,128]{2,1,0:T(8,128)(2,1)} %bitcast_select_fusion), calls=%async_computation.4 | async-start | bytes 65536 | tf_op jit(solution)/shard_map/all_to_all | solution.py:52
  210.9 24.8 %all-reduce.10.cloned.1.call-start = ((), (), s32[]{:S(2)}) async-start(), calls=%async_computation.9 | async-start | bytes 786432 | tf_op jit(solution)/shard_map/psum | solution.py:58
  220.7 84.3 %copy-start.27 = (s32[128]{0:T(128)}, s32[128]{0:T(128)S(1)}, u32[]{:S(2)}) copy-start(s32[128]{0:T(128)S(1)} %fusion.33) | copy-start | bytes 1540
  283.3 23.0 %copy-start.3 = (f32[2048,128]{0,1:T(8,128)S(1)}, f32[2048,128]{0,1:T(8,128)}, u32[]{:S(2)}) copy-start(f32[2048,128]{0,1:T(8,128)} %reduce-scatter.5.cloned.1.call-done) | copy-start | bytes 3145732
  283.3 23.0 %copy-start.24 = (f32[128]{0:T(128)S(1)}, f32[128]{0:T(128)}, u32[]{:S(2)}) copy-start(f32[128]{0:T(128)} %get-tuple-element.53) | copy-start | bytes 1540
  291.3 28.3 %copy-start.13 = (bf16[128,256]{1,0:T(8,128)(2,1)S(1)}, bf16[128,256]{1,0:T(8,128)(2,1)}, u32[]{:S(2)}) copy-start(bf16[128,256]{1,0:T(8,128)(2,1)} %squeeze.29) | copy-start | bytes 196612
  292.2 10.9 %all-to-all-start.3 = ((bf16[16,8,128]{2,1,0:T(8,128)(2,1)}), bf16[16,8,128]{2,1,0:T(8,128)(2,1)S(1)}, u32[]{:S(2)}, u32[]{:S(2)}) async-start(bf16[16,8,128]{2,1,0:T(8,128)(2,1)} %fusion.9), calls=%async_computation.5 | async-start | bytes 65536 | tf_op jit(solution)/shard_map/all_to_all | solution.py:100
  295.7 23.9 %all-gather.3.cloned.1.call-start = ((), (), s32[]{:S(2)}) async-start(), calls=%async_computation.10 | async-start | bytes 1572864 | tf_op jit(solution)/shard_map/all_gather | solution.py:161
  309.3 28.0 %copy-start.14 = (bf16[128,256]{1,0:T(8,128)(2,1)S(1)}, bf16[128,256]{1,0:T(8,128)(2,1)}, u32[]{:S(2)}) copy-start(bf16[128,256]{1,0:T(8,128)(2,1)} %squeeze.28) | copy-start | bytes 196612
  321.5 29.2 %copy-start.2 = (f32[2048,128]{0,1:T(8,128)S(1)}, f32[2048,128]{0,1:T(8,128)}, u32[]{:S(2)}) copy-start(f32[2048,128]{0,1:T(8,128)} %reduce-scatter.3.cloned.1.call-done) | copy-start | bytes 3145732
  321.6 29.2 %copy-start.22 = (f32[128]{0:T(128)S(1)}, f32[128]{0:T(128)}, u32[]{:S(2)}) copy-start(f32[128]{0:T(128)} %copy-done.21) | copy-start | bytes 1540
  330.3 33.4 %copy-start.5 = (bf16[2048,128]{0,1:T(8,128)(2,1)S(1)}, bf16[2048,128]{0,1:T(8,128)(2,1)}, u32[]{:S(2)}) copy-start(bf16[2048,128]{0,1:T(8,128)(2,1)} %copy-done.4) | copy-start | bytes 1572868
  330.3 14.3 %all-to-all-start.4 = ((bf16[16,8,128]{2,1,0:T(8,128)(2,1)}), bf16[16,8,128]{2,1,0:T(8,128)(2,1)S(1)}, u32[]{:S(2)}, u32[]{:S(2)}) async-start(bf16[16,8,128]{2,1,0:T(8,128)(2,1)} %fusion.10), calls=%async_computation.6 | async-start | bytes 65536 | tf_op jit(solution)/shard_map/all_to_all | solution.py:100
  337.3 28.4 %all-gather.5.cloned.1.call-start = ((), (), s32[]{:S(2)}) async-start(), calls=%async_computation.11 | async-start | bytes 1572864 | tf_op jit(solution)/shard_map/all_gather | solution.py:161
  350.7 18.6 %copy-start.25 = (f32[128]{0:T(128)S(1)}, f32[128]{0:T(128)}, u32[]{:S(2)}) copy-start(f32[128]{0:T(128)} %get-tuple-element.12) | copy-start | bytes 1540
  350.8 129.2 %copy-start.15 = (f32[1,6480]{1,0:T(1,128)S(1)}, f32[1,6480]{1,0:T(1,128)}, u32[]{:S(2)}) copy-start(f32[1,6480]{1,0:T(1,128)} %param.17) | copy-start | bytes 77764
  350.8 129.2 %copy-start.19 = (f32[1,6480]{1,0:T(1,128)S(1)}, f32[1,6480]{1,0:T(1,128)}, u32[]{:S(2)}) copy-start(f32[1,6480]{1,0:T(1,128)} %param.18) | copy-start | bytes 77764
  350.8 129.2 %copy-start.20 = (f32[1,6480]{1,0:T(1,128)S(1)}, f32[1,6480]{1,0:T(1,128)}, u32[]{:S(2)}) copy-start(f32[1,6480]{1,0:T(1,128)} %param.19) | copy-start | bytes 77764
  359.8 120.2 %all-reduce.12.cloned.1.call-start = ((), (), s32[]{:S(2)}) async-start(), calls=%async_computation.12 | async-start | bytes 829440 | tf_op jit(solution)/shard_map/psum | solution.py:176
  (8 other events, 72.3 us)
Sparse Core Ops, SparseCore 0:
  26.0 107.3 all-reduce.13
  138.7 9.3 reduce-scatter.2
  183.4 6.1 reduce-scatter.4
  220.6 15.0 all-reduce.9
  314.0 5.5 all-gather.2
  359.9 5.7 all-gather.4
  370.9 109.0 all-reduce.11
where the time goes:
time: 490 us; the launch traced here: 488 us
  waiting for transfers between devices  256 us (52%)
  matrix products  57.9 us (12%)
  blocking collectives  55.9 us (11%)
  other arithmetic  45.1 us (9%)
  starting transfers between devices  33.2 us (7%)
  local copies, waits for them, and re-layouts  24.5 us (5%)
  between operations  15.5 us (3%)
    psum x1, waiting for transfers between devices, per_device(): summed_all = lax.psum(gradient, 'dom')  109 us
    unnamed x8, waiting for transfers between devices  89.6 us
    psum x1, blocking collectives, per_device(): lax.psum((jnp.sum((log_total - picked) * weight_mask), jnp.sum(weight_mas...  42.6 us
    dot_general x12, matrix products, product(): return jnp.dot(matrix_a, matrix_b, preferred_element_type=jnp.float32)  26.4 us
    dot_general x10, matrix products, contract_rows(): lax.dot_general(matrix_a, matrix_b, (((0,), (0,)), ((), ())), preferred_e...  24.8 us
    all_to_all x3, starting transfers between devices, layer_forward(): lax.all_to_all(outgoing, 'dom', split_axis=0, concat_axis=0, tiled=True)  22 us
    psum x1, waiting for transfers between devices, layer_forward(): mixed = lax.psum(partial_value, 'feat')  15 us
    reduce_sum x2, other arithmetic, per_device(): degree = jnp.sum(local_mask, axis=1) + jnp.sum(halo_mask, axis=1)  13.9 us
  transfers between devices with their start and end apart: 12, of which 11 were waited for; matrix products, arithmetic and copies ran while one was open for 7% of the time, Pallas kernels for 0%

commit v1 on v0

--- a/solution.py
+++ b/solution.py
@@ -12,6 +12,17 @@
 DECAY_TWO = 0.999
 ADAM_EPS = 1e-08
 WEIGHT_DECAY = 0.01
+
+
+def cut_along(shard, dim, devices):
+    before, after = (shard.shape[:dim], shard.shape[dim + 1 :])
+    return jnp.moveaxis(shard.reshape(*before, devices, -1, *after), dim, 0)
+
+
+def laid_out(parts, dim):
+    parts = jnp.moveaxis(parts, 0, dim)
+    shape = parts.shape
+    return parts.reshape(*shape[:dim], shape[dim] * shape[dim + 1], *shape[dim + 2 :])
 
 
 def product(matrix_a, matrix_b):
@@ -49,7 +60,15 @@
 def layer_forward(states, weight_pair, graph, is_head):
     local_adj, halo_adj, inverse, send_index = graph
     outgoing = jnp.take(states, send_index, axis=0)
-    incoming = lax.all_to_all(outgoing, "dom", split_axis=0, concat_axis=0, tiled=True)
+    size, index = (lax.axis_size("dom"), lax.axis_index("dom"))
+    blocks = cut_along(outgoing, 0, size)
+    result = blocks
+    for turn in range(1, size):
+        target, source = ((index + turn) % size, (index - turn) % size)
+        sent = lax.dynamic_index_in_dim(blocks, target, 0)
+        other = lax.ppermute(sent, "dom", [(i, (i + turn) % size) for i in range(size)])
+        result = lax.dynamic_update_slice_in_dim(result, other, source, axis=0)
+    incoming = laid_out(result, 0)
     halo_feats = incoming.reshape(-1, states.shape[1])
     summed = product(local_adj, states) + product(halo_adj, halo_feats)
     aggregated = (summed * inverse[:, None]).astype(jnp.bfloat16)

time: 490 us -> 533 us (1.088); the launches traced: 488 us -> 525 us
  starting transfers between devices: 33.2 us -> 98.2 us
  waiting for transfers between devices: 256 us -> 234 us
    ppermute x0 -> x45, starting transfers between devices: none -> 87.5 us  [layer_forward(): lax.ppermute(sent, 'dom', [(i, (i + turn) % size) for i in range(size)])]
    unnamed x8, waiting for transfers between devices: 89.6 us -> 64.5 us
    all_to_all x3 -> x0, starting transfers between devices: 22 us -> none  [layer_forward(): lax.all_to_all(outgoing, 'dom', split_axis=0, concat_axis=0, tiled=True)]
    all_to_all x3 -> x0, waiting for transfers between devices: 12.9 us -> none  [layer_forward(): lax.all_to_all(outgoing, 'dom', split_axis=0, concat_axis=0, tiled=True)]
    reduce_scatter x2, waiting for transfers between devices: 11.7 us -> 18.7 us  [layer_forward(): lax.psum_scatter(partial_value, 'feat', scatter_dimension=1, tiled=True)]
  transfers between devices with their start and end apart: 12 -> 54, of which waited for: 11 -> 12; matrix products, arithmetic and copies ran while one was open for 7% -> 6% of each run, Pallas kernels for 0% -> 0%
where the time goes in v1:
time: 533 us; the launch traced here: 525 us
  waiting for transfers between devices  234 us (44%)
  starting transfers between devices  98.2 us (18%)
  blocking collectives  56.6 us (11%)
  matrix products  53.7 us (10%)
  other arithmetic  44 us (8%)
  local copies, waits for them, and re-layouts  21.6 us (4%)
  between operations  16.7 us (3%)
    psum x1, waiting for transfers between devices, per_device(): summed_all = lax.psum(gradient, 'dom')  110 us
    ppermute x45, starting transfers between devices, layer_forward(): lax.ppermute(sent, 'dom', [(i, (i + turn) % size) for i in range(size)])  87.5 us
    unnamed x8, waiting for transfers between devices  64.5 us
    psum x1, blocking collectives, per_device(): lax.psum((jnp.sum((log_total - picked) * weight_mask), jnp.sum(weight_mas...  42.6 us
    dot_general x10, matrix products, contract_rows(): lax.dot_general(matrix_a, matrix_b, (((0,), (0,)), ((), ())), preferred_e...  24.8 us
    dot_general x12, matrix products, product(): return jnp.dot(matrix_a, matrix_b, preferred_element_type=jnp.float32)  22.2 us
    psum x1, waiting for transfers between devices, layer_forward(): mixed = lax.psum(partial_value, 'feat')  20.1 us
    reduce_scatter x2, waiting for transfers between devices, layer_forward(): lax.psum_scatter(partial_value, 'feat', scatter_dimension=1, tiled=True)  18.7 us
  transfers between devices with their start and end apart: 54, of which 12 were waited for; matrix products, arithmetic and copies ran while one was open for 6% of the time, Pallas kernels for 0%

profile of v1, /device:TPU:0, one launch (start us, length us, event | category | flops | bytes accessed | tf_op | source)
XLA Modules:
  0.0 524.8 jit_solution(18136760847616767543)
XLA Ops:
  11.3 3.0 collective-permute-start
  25.7 13.5 %fusion.84 = (s32[2048]{0:T(1024)S(1)}, bf16[2048,2048]{1,0:T(8,128)(2,1)S(1)}) fusion(s32[2048,2048]{1,0:T(8,128)} %param.12), kind=kLoop, calls=%fused_computation.266 | loop fusion | flops 8386560 | bytes 25174016 | tf_op jit(solution)/shard_map/reduce_sum | solution.py:145
  46.5 4.4 collective-permute-start.6
  54.3 4.0 collective-permute-start.10
  61.6 3.6 collective-permute-start.14
  67.0 64.3 %all-reduce.14.cloned.1.call-done = bf16[103680]{0:T(1024)(128)(2,1)} async-done(((bf16[103680]{0:T(1024)(128)(2,1)}), bf16[103680]{0:T(1024)(128)(2,1)}) %all-reduce.14.cloned.1.call-update) | async-done | bytes 207376
  138.1 7.9 %reduce-scatter.3.cloned.1.call-done = f32[2048,128]{0,1:T(8,128)} async-done(((f32[2048,256]{0,1:T(8,128)}), f32[2048,128]{0,1:T(8,128)}) %reduce-scatter.3.cloned.1.call-update) | async-done | bytes 1048592 | tf_op jit(solution)/shard_map/reduce_scatter | solution.py:80
  147.3 3.8 all-reduce.5
  153.3 6.3 %fusion.88 = f32[128,2048]{1,0:T(8,128)S(1)} fusion(bf16[2048,128]{0,1:T(8,128)(2,1)S(1)} %multiply_convert_fusion.3, bf16[2048,2048]{1,0:T(8,128)(2,1)} %copy-done), kind=kOutput, calls=%fused_computation.270 | convolution fusion | flops 1073741824 | bytes 9961472 | tf_op jit(solution)/shard_map/dot_general | solution.py:29
  171.2 4.2 collective-permute-start.21
  178.9 4.1 collective-permute-start.25
  186.1 3.7 collective-permute-start.29
  194.8 10.8 %reduce-scatter.5.cloned.1.call-done = f32[2048,128]{0,1:T(8,128)} async-done(((f32[2048,256]{0,1:T(8,128)}), f32[2048,128]{0,1:T(8,128)}) %reduce-scatter.5.cloned.1.call-update) | async-done | bytes 1048592 | tf_op jit(solution)/shard_map/reduce_scatter | solution.py:80
  206.9 3.3 all-reduce.4
  212.4 6.3 %fusion.90 = f32[128,2048]{1,0:T(8,128)S(1)} fusion(bf16[2048,128]{0,1:T(8,128)(2,1)S(1)} %multiply_convert_fusion.2, bf16[2048,2048]{1,0:T(8,128)(2,1)} %copy-done), kind=kOutput, calls=%fused_computation.272 | convolution fusion | flops 1073741824 | bytes 9961472 | tf_op jit(solution)/shard_map/dot_general | solution.py:29
  230.1 4.2 collective-permute-start.36
  237.8 4.1 collective-permute-start.40
  245.1 3.9 collective-permute-start.44
  251.9 20.1 %all-reduce.10.cloned.1.call-done = f32[2048,47]{0,1:T(8,128)} async-done(((f32[2048,47]{0,1:T(8,128)}), f32[2048,47]{0,1:T(8,128)}) %all-reduce.10.cloned.1.call-update) | async-done | bytes 385040 | tf_op jit(solution)/shard_map/psum | solution.py:77
  274.8 42.6 %all-reduce.1 = (f32[]{:T(128)}, f32[]{:T(128)}) all-reduce(f32[]{:T(128)} %get-tuple-element.27, f32[]{:T(128)} %get-tuple-element.26), channel_id=1, replica_groups=mesh['dom'=16,'feat'=2] {'dom'}, use_global_device_ids=true, to_apply=%region_17.19 | all-reduce | flops 2 | bytes 16 | tf_op jit(solution)/shard_map/psum | solution.py:162
  319.6 7.9 %convolution_bitcast_fusion.2 = f32[2048,128]{1,0:T(8,128)} fusion(bf16[2048,128]{1,0:T(8,128)(2,1)S(1)} %fusion.5, bf16[2048,2048]{1,0:T(8,128)(2,1)} %copy-done), kind=kOutput, calls=%fused_computation.9 | convolution fusion | flops 1073741824 | bytes 9961472 | tf_op jit(solution)/shard_map/dot_general | solution.py:33
  328.5 3.5 all-to-all-start
  333.6 5.8 %all-to-all-done = bf16[16,8,128]{2,1,0:T(8,128)(2,1)S(1)} async-done(((bf16[16,8,128]{2,1,0:T(8,128)(2,1)}), bf16[16,8,128]{2,1,0:T(8,128)(2,1)S(1)}, u32[]{:S(2)}, u32[]{:S(2)}) %all-to-all-start) | async-done | bytes 32800 | tf_op jit(solution)/shard_map/all_to_all | solution.py:119
  345.4 3.6 all-reduce.3
  350.1 5.7 %all-gather.3.cloned.1.call-done = bf16[2048,256]{0,1:T(8,128)(2,1)} async-done(((bf16[2048,128]{0,1:T(8,128)(2,1)}), bf16[2048,256]{0,1:T(8,128)(2,1)}) %all-gather.3.cloned.1.call-update) | async-done | bytes 1048592 | tf_op jit(solution)/shard_map/all_gather | solution.py:180
  357.8 7.8 %convolution_bitcast_fusion.1 = f32[2048,128]{1,0:T(8,128)} fusion(bf16[2048,128]{1,0:T(8,128)(2,1)S(1)} %fusion.2, bf16[2048,2048]{1,0:T(8,128)(2,1)} %copy-done), kind=kOutput, calls=%fused_computation.8 | convolution fusion | flops 1073741824 | bytes 9961472 | tf_op jit(solution)/shard_map/dot_general | solution.py:33
  366.6 6.9 %all-to-all-start.1 = ((bf16[16,8,128]{2,1,0:T(8,128)(2,1)}), bf16[16,8,128]{2,1,0:T(8,128)(2,1)S(1)}, u32[]{:S(2)}, u32[]{:S(2)}) async-start(bf16[16,8,128]{2,1,0:T(8,128)(2,1)} %fusion.10), calls=%async_computation.3 | async-start | bytes 65536 | tf_op jit(solution)/shard_map/all_to_all | solution.py:119
  376.3 4.6 all-to-all-done.1
  380.9 3.5 scatter_custom_fusion.1
  387.0 3.3 multiply_reduce_fusion.1
  390.3 3.3 all-reduce.2
  406.6 109.6 %all-reduce.12.cloned.1.call-done = f32[1,103680]{1,0:T(1,128)} async-done(((f32[1,103680]{1,0:T(1,128)}), f32[1,103680]{1,0:T(1,128)}) %all-reduce.12.cloned.1.call-update) | async-done | bytes 414736 | tf_op jit(solution)/shard_map/psum | solution.py:195
  (305 shorter events, 124.7 us)
Async XLA Ops:
  7.2 124.2 %all-reduce.14.cloned.1.call-start = ((), (), s32[]{:S(2)}) async-start(), calls=%async_computation.10 | async-start | bytes 417792
  11.3 34.0 %collective-permute-start = (bf16[1,1,8,50]{3,2,0,1:T(8,128)(2,1)S(1)}, bf16[1,1,8,50]{3,2,0,1:T(8,128)(2,1)S(1)}, u32[]{:S(2)}, u32[]{:S(2)}) collective-permute-start(bf16[1,1,8,50]{3,2,0,1:T(8,128)(2,1)S(1)} %get-tuple-element.92), channel_id=1, source_target_pairs={{0,2},{2,4},{4,6},{6,8},{8,10},{10,12},{12,14},{14,16},{16,18},{18... | collective-permute-start | bytes 2408 | tf_op jit(solution)/shard_map/ppermute | solution.py:69
  14.2 32.3 %collective-permute-start.1 = (bf16[1,1,8,50]{3,2,0,1:T(8,128)(2,1)S(1)}, bf16[1,1,8,50]{3,2,0,1:T(8,128)(2,1)S(1)}, u32[]{:S(2)}, u32[]{:S(2)}) collective-permute-start(bf16[1,1,8,50]{3,2,0,1:T(8,128)(2,1)S(1)} %get-tuple-element.91), channel_id=1, source_target_pairs={{0,4},{2,6},{4,8},{6,10},{8,12},{10,14},{12,16},{14,18},{16,20},{1... | collective-permute-start | bytes 2408 | tf_op jit(solution)/shard_map/ppermute | solution.py:69
  15.8 35.1 %collective-permute-start.2 = (bf16[1,1,8,50]{3,2,0,1:T(8,128)(2,1)S(1)}, bf16[1,1,8,50]{3,2,0,1:T(8,128)(2,1)S(1)}, u32[]{:S(2)}, u32[]{:S(2)}) collective-permute-start(bf16[1,1,8,50]{3,2,0,1:T(8,128)(2,1)S(1)} %get-tuple-element.90), channel_id=1, source_target_pairs={{0,6},{2,8},{4,10},{6,12},{8,14},{10,16},{12,18},{14,20},{16,22},{... | collective-permute-start | bytes 2408 | tf_op jit(solution)/shard_map/ppermute | solution.py:69
  18.2 33.0 %collective-permute-start.3 = (bf16[1,1,8,50]{3,2,0,1:T(8,128)(2,1)S(1)}, bf16[1,1,8,50]{3,2,0,1:T(8,128)(2,1)S(1)}, u32[]{:S(2)}, u32[]{:S(2)}) collective-permute-start(bf16[1,1,8,50]{3,2,0,1:T(8,128)(2,1)S(1)} %get-tuple-element.89), channel_id=1, source_target_pairs={{0,8},{2,10},{4,12},{6,14},{8,16},{10,18},{12,20},{14,22},{16,24},... | collective-permute-start | bytes 2408 | tf_op jit(solution)/shard_map/ppermute | solution.py:69
  19.8 33.2 %collective-permute-start.4 = (bf16[1,1,8,50]{3,2,0,1:T(8,128)(2,1)S(1)}, bf16[1,1,8,50]{3,2,0,1:T(8,128)(2,1)S(1)}, u32[]{:S(2)}, u32[]{:S(2)}) collective-permute-start(bf16[1,1,8,50]{3,2,0,1:T(8,128)(2,1)S(1)} %get-tuple-element.88), channel_id=1, source_target_pairs={{0,10},{2,12},{4,14},{6,16},{8,18},{10,20},{12,22},{14,24},{16,26}... | collective-permute-start | bytes 2408 | tf_op jit(solution)/shard_map/ppermute | solution.py:69
  25.2 120.7 %reduce-scatter.3.cloned.1.call-start = ((), (), s32[]{:S(2)}) async-start(), calls=%async_computation.4 | async-start | bytes 3145728 | tf_op jit(solution)/shard_map/reduce_scatter | solution.py:80
  46.5 11.8 %collective-permute-start.6 = (bf16[1,1,8,50]{3,2,0,1:T(8,128)(2,1)S(1)}, bf16[1,1,8,50]{3,2,0,1:T(8,128)(2,1)S(1)}, u32[]{:S(2)}, u32[]{:S(2)}) collective-permute-start(bf16[1,1,8,50]{3,2,0,1:T(8,128)(2,1)S(1)} %get-tuple-element.86), channel_id=1, source_target_pairs={{0,14},{2,16},{4,18},{6,20},{8,22},{10,24},{12,26},{14,28},{16,30}... | collective-permute-start | bytes 2408 | tf_op jit(solution)/shard_map/ppermute | solution.py:69
  50.9 9.2 %collective-permute-start.7 = (bf16[1,1,8,50]{3,2,0,1:T(8,128)(2,1)S(1)}, bf16[1,1,8,50]{3,2,0,1:T(8,128)(2,1)S(1)}, u32[]{:S(2)}, u32[]{:S(2)}) collective-permute-start(bf16[1,1,8,50]{3,2,0,1:T(8,128)(2,1)S(1)} %get-tuple-element.85), channel_id=1, source_target_pairs={{0,16},{2,18},{4,20},{6,22},{8,24},{10,26},{12,28},{14,30},{16,0},... | collective-permute-start | bytes 2408 | tf_op jit(solution)/shard_map/ppermute | solution.py:69
  54.3 11.0 %collective-permute-start.10 = (bf16[1,1,8,50]{3,2,0,1:T(8,128)(2,1)S(1)}, bf16[1,1,8,50]{3,2,0,1:T(8,128)(2,1)S(1)}, u32[]{:S(2)}, u32[]{:S(2)}) collective-permute-start(bf16[1,1,8,50]{3,2,0,1:T(8,128)(2,1)S(1)} %get-tuple-element.82), channel_id=1, source_target_pairs={{0,22},{2,24},{4,26},{6,28},{8,30},{10,0},{12,2},{14,4},{16,6},{18... | collective-permute-start | bytes 2408 | tf_op jit(solution)/shard_map/ppermute | solution.py:69
  136.5 69.1 %reduce-scatter.5.cloned.1.call-start = ((), (), s32[]{:S(2)}) async-start(), calls=%async_computation.5 | async-start | bytes 3145728 | tf_op jit(solution)/shard_map/reduce_scatter | solution.py:80
  160.4 9.3 %collective-permute-start.15 = (bf16[1,1,8,128]{3,2,0,1:T(8,128)(2,1)S(1)}, bf16[1,1,8,128]{3,2,0,1:T(8,128)(2,1)S(1)}, u32[]{:S(2)}, u32[]{:S(2)}) collective-permute-start(bf16[1,1,8,128]{3,2,0,1:T(8,128)(2,1)S(1)} %get-tuple-element.77), channel_id=1, source_target_pairs={{0,2},{2,4},{4,6},{6,8},{8,10},{10,12},{12,14},{14,16},{16,18},{18... | collective-permute-start | bytes 6152 | tf_op jit(solution)/shard_map/ppermute | solution.py:69
  163.8 11.6 %collective-permute-start.17 = (bf16[1,1,8,128]{3,2,0,1:T(8,128)(2,1)S(1)}, bf16[1,1,8,128]{3,2,0,1:T(8,128)(2,1)S(1)}, u32[]{:S(2)}, u32[]{:S(2)}) collective-permute-start(bf16[1,1,8,128]{3,2,0,1:T(8,128)(2,1)S(1)} %get-tuple-element.75), channel_id=1, source_target_pairs={{0,6},{2,8},{4,10},{6,12},{8,14},{10,16},{12,18},{14,20},{16,22},{... | collective-permute-start | bytes 6152 | tf_op jit(solution)/shard_map/ppermute | solution.py:69
  166.1 9.8 %collective-permute-start.18 = (bf16[1,1,8,128]{3,2,0,1:T(8,128)(2,1)S(1)}, bf16[1,1,8,128]{3,2,0,1:T(8,128)(2,1)S(1)}, u32[]{:S(2)}, u32[]{:S(2)}) collective-permute-start(bf16[1,1,8,128]{3,2,0,1:T(8,128)(2,1)S(1)} %get-tuple-element.74), channel_id=1, source_target_pairs={{0,8},{2,10},{4,12},{6,14},{8,16},{10,18},{12,20},{14,22},{16,24},... | collective-permute-start | bytes 6152 | tf_op jit(solution)/shard_map/ppermute | solution.py:69
  167.6 9.8 %collective-permute-start.19 = (bf16[1,1,8,128]{3,2,0,1:T(8,128)(2,1)S(1)}, bf16[1,1,8,128]{3,2,0,1:T(8,128)(2,1)S(1)}, u32[]{:S(2)}, u32[]{:S(2)}) collective-permute-start(bf16[1,1,8,128]{3,2,0,1:T(8,128)(2,1)S(1)} %get-tuple-element.73), channel_id=1, source_target_pairs={{0,10},{2,12},{4,14},{6,16},{8,18},{10,20},{12,22},{14,24},{16,26}... | collective-permute-start | bytes 6152 | tf_op jit(solution)/shard_map/ppermute | solution.py:69
  169.7 9.2 %collective-permute-start.20 = (bf16[1,1,8,128]{3,2,0,1:T(8,128)(2,1)S(1)}, bf16[1,1,8,128]{3,2,0,1:T(8,128)(2,1)S(1)}, u32[]{:S(2)}, u32[]{:S(2)}) collective-permute-start(bf16[1,1,8,128]{3,2,0,1:T(8,128)(2,1)S(1)} %get-tuple-element.72), channel_id=1, source_target_pairs={{0,12},{2,14},{4,16},{6,18},{8,20},{10,22},{12,24},{14,26},{16,28}... | collective-permute-start | bytes 6152 | tf_op jit(solution)/shard_map/ppermute | solution.py:69
  171.2 11.8 %collective-permute-start.21 = (bf16[1,1,8,128]{3,2,0,1:T(8,128)(2,1)S(1)}, bf16[1,1,8,128]{3,2,0,1:T(8,128)(2,1)S(1)}, u32[]{:S(2)}, u32[]{:S(2)}) collective-permute-start(bf16[1,1,8,128]{3,2,0,1:T(8,128)(2,1)S(1)} %get-tuple-element.71), channel_id=1, source_target_pairs={{0,14},{2,16},{4,18},{6,20},{8,22},{10,24},{12,26},{14,28},{16,30}... | collective-permute-start | bytes 6152 | tf_op jit(solution)/shard_map/ppermute | solution.py:69
  175.4 9.2 %collective-permute-start.22 = (bf16[1,1,8,128]{3,2,0,1:T(8,128)(2,1)S(1)}, bf16[1,1,8,128]{3,2,0,1:T(8,128)(2,1)S(1)}, u32[]{:S(2)}, u32[]{:S(2)}) collective-permute-start(bf16[1,1,8,128]{3,2,0,1:T(8,128)(2,1)S(1)} %get-tuple-element.70), channel_id=1, source_target_pairs={{0,16},{2,18},{4,20},{6,22},{8,24},{10,26},{12,28},{14,30},{16,0},... | collective-permute-start | bytes 6152 | tf_op jit(solution)/shard_map/ppermute | solution.py:69
  178.9 11.0 %collective-permute-start.25 = (bf16[1,1,8,128]{3,2,0,1:T(8,128)(2,1)S(1)}, bf16[1,1,8,128]{3,2,0,1:T(8,128)(2,1)S(1)}, u32[]{:S(2)}, u32[]{:S(2)}) collective-permute-start(bf16[1,1,8,128]{3,2,0,1:T(8,128)(2,1)S(1)} %get-tuple-element.67), channel_id=1, source_target_pairs={{0,22},{2,24},{4,26},{6,28},{8,30},{10,0},{12,2},{14,4},{16,6},{18... | collective-permute-start | bytes 6152 | tf_op jit(solution)/shard_map/ppermute | solution.py:69
  194.2 77.8 %all-reduce.10.cloned.1.call-start = ((), (), s32[]{:S(2)}) async-start(), calls=%async_computation.6 | async-start | bytes 786432 | tf_op jit(solution)/shard_map/psum | solution.py:77
  222.9 11.4 %collective-permute-start.32 = (bf16[1,1,8,128]{3,2,0,1:T(8,128)(2,1)S(1)}, bf16[1,1,8,128]{3,2,0,1:T(8,128)(2,1)S(1)}, u32[]{:S(2)}, u32[]{:S(2)}) collective-permute-start(bf16[1,1,8,128]{3,2,0,1:T(8,128)(2,1)S(1)} %get-tuple-element.60), channel_id=1, source_target_pairs={{0,6},{2,8},{4,10},{6,12},{8,14},{10,16},{12,18},{14,20},{16,22},{... | collective-permute-start | bytes 6152 | tf_op jit(solution)/shard_map/ppermute | solution.py:69
  225.3 9.5 %collective-permute-start.33 = (bf16[1,1,8,128]{3,2,0,1:T(8,128)(2,1)S(1)}, bf16[1,1,8,128]{3,2,0,1:T(8,128)(2,1)S(1)}, u32[]{:S(2)}, u32[]{:S(2)}) collective-permute-start(bf16[1,1,8,128]{3,2,0,1:T(8,128)(2,1)S(1)} %get-tuple-element.59), channel_id=1, source_target_pairs={{0,8},{2,10},{4,12},{6,14},{8,16},{10,18},{12,20},{14,22},{16,24},... | collective-permute-start | bytes 6152 | tf_op jit(solution)/shard_map/ppermute | solution.py:69
  226.8 9.6 %collective-permute-start.34 = (bf16[1,1,8,128]{3,2,0,1:T(8,128)(2,1)S(1)}, bf16[1,1,8,128]{3,2,0,1:T(8,128)(2,1)S(1)}, u32[]{:S(2)}, u32[]{:S(2)}) collective-permute-start(bf16[1,1,8,128]{3,2,0,1:T(8,128)(2,1)S(1)} %get-tuple-element.58), channel_id=1, source_target_pairs={{0,10},{2,12},{4,14},{6,16},{8,18},{10,20},{12,22},{14,24},{16,26}... | collective-permute-start | bytes 6152 | tf_op jit(solution)/shard_map/ppermute | solution.py:69
  228.6 9.2 %collective-permute-start.35 = (bf16[1,1,8,128]{3,2,0,1:T(8,128)(2,1)S(1)}, bf16[1,1,8,128]{3,2,0,1:T(8,128)(2,1)S(1)}, u32[]{:S(2)}, u32[]{:S(2)}) collective-permute-start(bf16[1,1,8,128]{3,2,0,1:T(8,128)(2,1)S(1)} %get-tuple-element.57), channel_id=1, source_target_pairs={{0,12},{2,14},{4,16},{6,18},{8,20},{10,22},{12,24},{14,26},{16,28}... | collective-permute-start | bytes 6152 | tf_op jit(solution)/shard_map/ppermute | solution.py:69
  230.1 11.9 %collective-permute-start.36 = (bf16[1,1,8,128]{3,2,0,1:T(8,128)(2,1)S(1)}, bf16[1,1,8,128]{3,2,0,1:T(8,128)(2,1)S(1)}, u32[]{:S(2)}, u32[]{:S(2)}) collective-permute-start(bf16[1,1,8,128]{3,2,0,1:T(8,128)(2,1)S(1)} %get-tuple-element.56), channel_id=1, source_target_pairs={{0,14},{2,16},{4,18},{6,20},{8,22},{10,24},{12,26},{14,28},{16,30}... | collective-permute-start | bytes 6152 | tf_op jit(solution)/shard_map/ppermute | solution.py:69
  234.3 9.2 %collective-permute-start.37 = (bf16[1,1,8,128]{3,2,0,1:T(8,128)(2,1)S(1)}, bf16[1,1,8,128]{3,2,0,1:T(8,128)(2,1)S(1)}, u32[]{:S(2)}, u32[]{:S(2)}) collective-permute-start(bf16[1,1,8,128]{3,2,0,1:T(8,128)(2,1)S(1)} %get-tuple-element.55), channel_id=1, source_target_pairs={{0,16},{2,18},{4,20},{6,22},{8,24},{10,26},{12,28},{14,30},{16,0},... | collective-permute-start | bytes 6152 | tf_op jit(solution)/shard_map/ppermute | solution.py:69
  237.8 11.1 %collective-permute-start.40 = (bf16[1,1,8,128]{3,2,0,1:T(8,128)(2,1)S(1)}, bf16[1,1,8,128]{3,2,0,1:T(8,128)(2,1)S(1)}, u32[]{:S(2)}, u32[]{:S(2)}) collective-permute-start(bf16[1,1,8,128]{3,2,0,1:T(8,128)(2,1)S(1)} %get-tuple-element.52), channel_id=1, source_target_pairs={{0,22},{2,24},{4,26},{6,28},{8,30},{10,0},{12,2},{14,4},{16,6},{18... | collective-permute-start | bytes 6152 | tf_op jit(solution)/shard_map/ppermute | solution.py:69
  328.5 10.9 %all-to-all-start = ((bf16[16,8,128]{2,1,0:T(8,128)(2,1)}), bf16[16,8,128]{2,1,0:T(8,128)(2,1)S(1)}, u32[]{:S(2)}, u32[]{:S(2)}) async-start(bf16[16,8,128]{2,1,0:T(8,128)(2,1)} %fusion.9), calls=%async_computation.2 | async-start | bytes 65536 | tf_op jit(solution)/shard_map/all_to_all | solution.py:119
  332.0 23.8 %all-gather.3.cloned.1.call-start = ((), (), s32[]{:S(2)}) async-start(), calls=%async_computation.7 | async-start | bytes 1572864 | tf_op jit(solution)/shard_map/all_gather | solution.py:180
  366.6 14.3 %all-to-all-start.1 = ((bf16[16,8,128]{2,1,0:T(8,128)(2,1)}), bf16[16,8,128]{2,1,0:T(8,128)(2,1)S(1)}, u32[]{:S(2)}, u32[]{:S(2)}) async-start(bf16[16,8,128]{2,1,0:T(8,128)(2,1)} %fusion.10), calls=%async_computation.3 | async-start | bytes 65536 | tf_op jit(solution)/shard_map/all_to_all | solution.py:119
  373.5 28.3 %all-gather.5.cloned.1.call-start = ((), (), s32[]{:S(2)}) async-start(), calls=%async_computation.8 | async-start | bytes 1572864 | tf_op jit(solution)/shard_map/all_gather | solution.py:180
  396.0 120.2 %all-reduce.12.cloned.1.call-start = ((), (), s32[]{:S(2)}) async-start(), calls=%async_computation.9 | async-start | bytes 829440 | tf_op jit(solution)/shard_map/psum | solution.py:195
  (51 other events, 1499.8 us)
Sparse Core Ops, SparseCore 0:
  25.4 105.9 all-reduce.13
  136.6 9.3 reduce-scatter.2
  194.3 11.2 reduce-scatter.4
  251.8 20.1 all-reduce.9
  350.3 5.5 all-gather.2
  396.1 5.6 all-gather.4
  407.0 109.1 all-reduce.11
